TPU v7x, 32 devices: a whole 2x2x4 slice. The times are simulated.
32 devices in a mesh: groups: 2 (over x), tensor: 16 (over z, y, core).
Axes of the slice: x: 2, y: 2, z: 4, core: 2. Of those that a mesh axis runs over, the one named last changes fastest.
Arguments:
- residual_input: bfloat16 [2, 512, 8192], P(None, 'groups', 'tensor'), parts along dimension 1, may hold values from -6 to 6
- gain: bfloat16 [8192], P('tensor'), may hold values from 0.099609375 to 1.8984375
- gate_up_weight: bfloat16 [8192, 2, 14336], P(None, None, 'tensor'), may hold values from -0.0625 to 0.0625
- adapter_down_maps: bfloat16 [8192, 16, 128], P('tensor'), may hold values from -0.0625 to 0.0625
- adapter_up_maps: bfloat16 [16, 2, 64, 14336], P('tensor'), may hold values from -0.75 to 0.75
- row_adapter_index: int32 [2, 512, 1], P(None, 'groups'), parts along dimension 1, may hold values from 0 to 15; in each aligned block of 256 rows (0 to 255, 256 to 511, ..., all dimensions but the last counted through in order) at most 16 rows name the same one
- adapter_storage_slot: int32 [16], replicated, may hold values from 0 to 15, each once
Outputs:
- hidden_out: bfloat16 [2, 512, 14336], P(None, 'groups', 'tensor'), parts along dimension 1
There are 2 independent parts, one for each index of `groups`. A program takes and returns all parts, laid end to end along the dimension named above; an argument that names none is the same for every part. Nothing has to cross between parts.
Inputs may be any that keep to these rules, and one draw needn't show every extreme that they name: `row_adapter_index`: within one decode step at most 16 rows name the same adapter, and in some step one adapter is named by exactly 16 rows. `adapter_storage_slot`: each slot is used by exactly one adapter.
All inputs are finite; a program needn't handle non-finite values.
Results may differ from a plain program's by a relative error of at most 0.0079.
Values may be sent and summed in bfloat16 or wider, within the bound.
A program may use at most 256 MiB of HBM per device.

v0:
```python
import jax
import jax.numpy as jnp
from jax import lax
from jax.sharding import PartitionSpec as P


def per_device(
    residual_input,
    gain,
    gate_up_weight,
    adapter_down_maps,
    adapter_up_maps,
    row_adapter_index,
    adapter_storage_slot,
):
    steps_count, rows_count, local_width = residual_input.shape
    local_ff = gate_up_weight.shape[2]
    adapter_total = adapter_down_maps.shape[1]
    paired_rank = adapter_down_maps.shape[2]
    rank = paired_rank // 2
    total_rows = steps_count * rows_count
    flat = residual_input.reshape(total_rows, local_width)
    weights_flat = gate_up_weight.reshape(gate_up_weight.shape[0], 2 * local_ff)
    whole, full_gain = (
        lax.all_gather(flat, "tensor", axis=1, tiled=True),
        lax.all_gather(gain, "tensor", axis=0, tiled=True),
    )
    wide = whole.astype(jnp.float32)
    rstd = lax.rsqrt(jnp.mean(wide * wide, axis=1, keepdims=True) + 1e-05)
    normed_full = (wide * rstd * full_gain.astype(jnp.float32)).astype(jnp.bfloat16)
    base_output = jnp.dot(normed_full, weights_flat, preferred_element_type=jnp.float32)
    offset = lax.axis_index("tensor") * local_width
    normed_input = lax.dynamic_slice_in_dim(normed_full, offset, local_width, 1)
    base_output = base_output.reshape(total_rows, 2, local_ff)
    ids = row_adapter_index.reshape(total_rows)
    ad_range = jnp.arange(adapter_total, dtype=jnp.int32)
    pick_int = (ids[:, None] == ad_range[None, :]).astype(jnp.int32)
    every_slot = jnp.dot(
        normed_input,
        adapter_down_maps.reshape(local_width, adapter_total * paired_rank),
        preferred_element_type=jnp.float32,
    )
    every_slot = every_slot.reshape(total_rows, adapter_total, paired_rank)
    partial_sum = jnp.einsum("na,nar->nr", pick_int.astype(jnp.float32), every_slot)
    shrink_output = lax.psum(partial_sum, "tensor").astype(jnp.bfloat16)
    storage_slot = jnp.sum(pick_int * adapter_storage_slot[None, :], axis=1)
    slot_hot = storage_slot[:, None] == ad_range[None, :]
    fetched_maps = lax.all_to_all(
        adapter_up_maps, "tensor", split_axis=3, concat_axis=0, tiled=True
    )
    slot_mask = slot_hot.astype(jnp.bfloat16)
    adapter_terms = []
    for half in range(2):
        values = shrink_output[:, half * rank : (half + 1) * rank]
        masked = (slot_mask[:, :, None] * values[:, None, :]).reshape(
            total_rows, adapter_total * rank
        )
        slot_maps = fetched_maps[:, half].reshape(adapter_total * rank, local_ff)
        adapter_terms.append(jnp.dot(masked, slot_maps, preferred_element_type=jnp.float32))
    adapter_output = jnp.stack(adapter_terms, axis=1).astype(jnp.bfloat16)
    adapter_wide_output = adapter_output.astype(jnp.float32)
    gate_output = base_output[:, 0, :] + 2.0 * adapter_wide_output[:, 0, :]
    upper_output = base_output[:, 1, :] + 2.0 * adapter_wide_output[:, 1, :]
    result = (jax.nn.silu(gate_output) * upper_output).astype(jnp.bfloat16)
    return result.reshape(steps_count, rows_count, local_ff)


def solution(mesh):
    return jax.shard_map(
        per_device,
        mesh=mesh,
        in_specs=(
            P(None, "groups", "tensor"),
            P("tensor"),
            P(None, None, "tensor"),
            P("tensor", None, None),
            P("tensor", None, None, None),
            P(None, "groups", None),
            P(),
        ),
        out_specs=P(None, "groups", "tensor"),
        check_vma=False,
    )
```

profile of v0, /device:TPU:0, one launch (start us, length us, event | category | flops | bytes accessed | tf_op | source)
XLA Modules:
  0.0 376.7 jit_solution(2295217125544517508)
XLA Ops:
  6.5 0.7 all-gather.3.cloned.1.call-update
  7.3 15.8 %copy.22 = bf16[1,2,64,14336]{2,1,0,3:T(2,128)(2,1)} copy(bf16[1,2,64,14336]{3,2,1,0:T(8,128)(2,1)} %param.11) | data formatting | bytes 7340032 | tf_op args[4]
  23.1 13.3 %reshape.95 = bf16[16,2,57344]{2,1,0:T(2,128)(2,1)} reshape(bf16[14336,1,2,64]{3,2,1,0:T(2,128)(2,1)} %bitcast.48) | data formatting | bytes 7340032
  36.4 7.6 %all-to-all-start = ((bf16[16,2,57344]{2,1,0:T(2,128)(2,1)}), bf16[16,2,57344]{2,1,0:T(2,128)(2,1)}, u32[]{:S(2)}, u32[]{:S(2)}) async-start(bf16[16,2,57344]{2,1,0:T(2,128)(2,1)} %reshape.95), calls=%async_computation | async-start | bytes 7340032 | tf_op jit(solution)/shard_map/all_to_all | solution.py:48
  44.0 109.4 %all-gather = bf16[16,1,512]{2,1,0:T(2,128)(2,1)S(1)} all-gather(bf16[1,1,512]{2,1,0:T(2,128)(2,1)S(1)} %reshape.88), channel_id=1, replica_groups=mesh['groups'=2,'tensor'=16] {'tensor'}, dimensions={0}, use_global_device_ids=true | all-gather | bytes 17408 | tf_op jit(solution)/shard_map/all_gather | solution.py:26
  153.5 2.1 copy.35
  155.6 2.5 copy.21
  158.2 20.0 %copy.32 = bf16[1024,8,2,896]{3,1,2,0:T(8,128)(2,1)} copy(bf16[1024,8,2,896]{3,2,1,0:T(2,128)(2,1)} %bitcast.45) | data formatting | bytes 58720256
  178.2 39.4 %copy.20 = bf16[1792,8192]{1,0:T(8,128)(2,1)} copy(bf16[1792,8192]{0,1:T(8,128)(2,1)} %bitcast.44) | data formatting | bytes 58720256 | tf_op jit(solution)/shard_map/dot_general | solution.py:31
  217.8 13.0 %reshape.96 = bf16[14336,1,2,64]{3,2,1,0:T(2,128)(2,1)} reshape(bf16[16,2,57344]{2,1,0:T(2,128)(2,1)} %all-to-all-done) | data formatting | bytes 7340032
  230.8 12.1 %copy.31 = bf16[1,2,64,16,896]{4,3,2,1,0:T(8,128)(2,1)} copy(bf16[1,2,64,16,896]{2,1,4,3,0:T(2,128)(2,1)} %bitcast.47) | data formatting | bytes 7340032 | tf_op jit(solution)/shard_map/all_to_all | solution.py:48
  242.8 2.3 fusion.13
  245.2 1.7 copy.24
  246.9 0.4 copy.25
  247.3 5.1 %fusion = f32[512]{0:T(512)S(1)} fusion(bf16[512,8192]{1,0:T(8,128)(2,1)} %all-gather.3.cloned.1.call-done), kind=kLoop, calls=%fused_computation.2 | loop fusion | flops 12582400 | bytes 8390656 | tf_op jit(solution)/shard_map/reduce_sum | solution.py:29
  252.4 10.1 %fusion.2 = bf16[512,8192]{1,0:T(8,128)(2,1)} fusion(bf16[512,8192]{1,0:T(8,128)(2,1)} %all-gather.3.cloned.1.call-done, f32[8192]{0:T(1024)S(1)} %bitcast.60, f32[512]{0:T(512)S(1)} %add_rsqrt_fusion), kind=kLoop, calls=%fused_computation.4 | loop fusion | flops 16777216 | bytes 16812032 | tf_op jit(solution)/shard_map/convert_element_type | solution.py:30
  262.5 2.6 multiply_reduce_fusion
  265.3 78.4 %all-reduce.1 = bf16[512,128]{0,1:T(8,128)(2,1)S(1)} all-reduce(f32[512,128]{0,1:T(8,128)S(1)} %copy.30), channel_id=1, replica_groups=mesh['groups'=2,'tensor'=16] {'tensor'}, use_global_device_ids=true, to_apply=%region_2.0 | all-reduce | flops 65536 | bytes 393216 | tf_op jit(solution)/shard_map/psum | solution.py:45
  343.7 19.9 %fusion.3 = f32[512,2,896]{2,0,1:T(8,128)S(1)} fusion(bf16[2,896,8192]{2,1,0:T(8,128)(2,1)} %bitcast.46, bf16[512,8192]{1,0:T(8,128)(2,1)} %fusion.2), kind=kOutput, calls=%fused_computation.5 | convolution fusion | flops 15032385536 | bytes 41418752 | tf_op jit(solution)/shard_map/dot_general | solution.py:31
  363.8 1.3 copy-done.1
  365.1 1.3 fusion.7
  366.4 1.3 fusion.8
  367.9 0.5 fusion.6
  368.4 1.5 multiply_convert_fusion
  (22 shorter events, 0.7 us)
Async XLA Ops:
  6.5 240.8 %all-gather.3.cloned.1.call-start = ((), (), s32[]{:S(2)}) async-start(), calls=%async_computation.1 | async-start | bytes 8912896 | tf_op jit(solution)/shard_map/all_gather | solution.py:25
  36.4 7.6 %copy-start.3 = (bf16[512]{0:T(512)(128)(2,1)S(1)}, bf16[512]{0:T(512)(128)(2,1)}, u32[]{:S(2)}) copy-start(bf16[512]{0:T(512)(128)(2,1)} %param.8) | copy-start | bytes 3076
  36.4 181.3 %all-to-all-start = ((bf16[16,2,57344]{2,1,0:T(2,128)(2,1)}), bf16[16,2,57344]{2,1,0:T(2,128)(2,1)}, u32[]{:S(2)}, u32[]{:S(2)}) async-start(bf16[16,2,57344]{2,1,0:T(2,128)(2,1)} %reshape.95), calls=%async_computation | async-start | bytes 7340032 | tf_op jit(solution)/shard_map/all_to_all | solution.py:48
  178.2 39.5 %copy-start.2 = (s32[2,256,1]{1,2,0:T(1,128)S(1)}, s32[2,256,1]{1,2,0:T(1,128)}, u32[]{:S(2)}) copy-start(s32[2,256,1]{1,2,0:T(1,128)} %param.12) | copy-start | bytes 6148
  178.2 39.5 %copy-start.4 = (s32[16]{0:T(128)S(1)}, s32[16]{0:T(128)}, u32[]{:S(2)}) copy-start(s32[16]{0:T(128)} %param.13) | copy-start | bytes 196
  252.4 10.1 %copy-start = (bf16[2048,512]{1,0:T(8,128)(2,1)S(1)}, bf16[2048,512]{1,0:T(8,128)(2,1)}, u32[]{:S(2)}) copy-start(bf16[2048,512]{1,0:T(8,128)(2,1)} %copy.21) | copy-start | bytes 6291460
  363.6 1.5 copy-start.1
Sparse Core Ops, SparseCore 0:
  9.5 132.7 all-gather.2
where the time goes:
time: 379 us; the launch traced here: 377 us
  blocking collectives  188 us (50%)
  local copies, waits for them, and re-layouts  124 us (33%)
  matrix products  25.1 us (7%)
  other arithmetic  17.7 us (5%)
  between operations  13.5 us (4%)
  starting transfers between devices  7.58 us (2%)
    all_gather x1, blocking collectives, per_device(): lax.all_gather(gain, 'tensor', axis=0, tiled=True)  109 us
    psum x1, blocking collectives, per_device(): shrink_output = lax.psum(partial_sum, 'tensor').astype(jnp.bfloat16)  78.4 us
    unnamed x16, local copies, waits for them, and re-layouts  65.7 us
    dot_general x1, local copies, waits for them, and re-layouts, per_device(): jnp.dot(normed_full, weights_flat, preferred_element_type=jnp.float32)  39.4 us
    dot_general x1, matrix products, per_device(): jnp.dot(normed_full, weights_flat, preferred_element_type=jnp.float32)  19.9 us
    all_to_all x1, local copies, waits for them, and re-layouts, per_device(): lax.all_to_all(adapter_up_maps, 'tensor', split_axis=3, concat_axis=0, ti...  12.1 us
    convert_element_type x1, other arithmetic, per_device(): (wide * rstd * full_gain.astype(jnp.float32)).astype(jnp.bfloat16)  10.1 us
  transfers between devices with their start and end apart: 2, of which 0 were waited for; matrix products, arithmetic and copies ran while one was open for 33% of the time, Pallas kernels for 0%

commit v1 on v0

v1 whole, which is shorter than its diff:
```python
import functools
import jax
import jax.numpy as jnp
from jax import lax
from jax.experimental import pallas as pl
from jax.experimental.pallas import tpu as pltpu
from jax.sharding import PartitionSpec as P

CAP = 16
MESH = pl.DeviceIdType.MESH


def exchange(n, ny, lf, wide, xg, ssq, sp, up, xall, ssq_all, lora_all,
             sp_all, lora_buf, x_send, x_recv, q_send, q_recv, s_send, s_recv,
             l_send, l_recv, own_sem):
    nz = n // (2 * ny)
    me = lax.axis_index("tensor")
    core = lax.rem(me, 2)
    y = lax.rem(me // 2, ny)
    z = me // (2 * ny)
    half = up.shape[-2]

    def index(zz, yy, cc):
        return (zz * ny + yy) * 2 + cc

    barrier = pltpu.get_barrier_semaphore()

    @pl.loop(1, n)
    def _(d):
        pl.semaphore_signal(barrier, inc=1, device_id={"tensor": lax.rem(me + d, n)},
                            device_id_type=MESH)

    pl.semaphore_wait(barrier, n - 1)

    def remote(src, dst, send, recv, peer):
        return pltpu.make_async_remote_copy(
            src_ref=src, dst_ref=dst, send_sem=send, recv_sem=recv,
            device_id={"tensor": peer}, device_id_type=MESH)

    def sp_copy(peer, slot):
        return remote(sp.at[peer], sp_all.at[slot], s_send.at[peer], s_recv.at[slot], peer)

    def ssq_copy(peer, slot):
        return remote(ssq, ssq_all.at[slot], q_send.at[peer], q_recv.at[slot], peer)

    def lora_copy(peer, slot):
        return remote(lora_buf.at[peer], lora_all.at[slot], l_send.at[peer],
                      l_recv.at[slot], peer)

    def x_copy(src, way, block, peer):
        return remote(src, xall.at[block], x_send.at[way, block], x_recv.at[block], peer)

    def sends(block, src, act, up_way, down_way, y_way):
        if up_way is not None:
            @pl.when(jnp.logical_and(up_way, z + 1 < nz))
            def _():
                act(x_copy(src, 0, block, lax.rem(index(z + 1, y, core), n)))
        if down_way is not None:
            @pl.when(jnp.logical_and(down_way, z > 0))
            def _():
                act(x_copy(src, 1, block, lax.rem(index(z - 1, y, core) + n, n)))
        if y_way and ny == 2:
            act(x_copy(src, 2, block, index(z, 1 - y, core)))
        act(x_copy(src, 3, block, index(z, y, 1 - core)))

    def begin(copy):
        copy.start()

    @pl.loop(1, n)
    def _(d):
        sp_copy(lax.rem(me + d, n), me).start()

    yes = z >= 0
    sends(me, xg, begin, yes, yes, True)

    @pl.loop(1, n)
    def _(d):
        ssq_copy(lax.rem(me + d, n), me).start()

    own = [pltpu.make_async_copy(sp.at[me], sp_all.at[me], own_sem.at[0]),
           pltpu.make_async_copy(ssq, ssq_all.at[me], own_sem.at[1]),
           pltpu.make_async_copy(xg, xall.at[me], own_sem.at[2])]
    for copy in own:
        copy.start()
    own[0].wait()

    @pl.loop(1, n)
    def _(d):
        peer = lax.rem(me + d, n)
        sp_copy(peer, peer).wait_recv()

    shrink = jnp.sum(sp_all[...], axis=0).astype(jnp.bfloat16)

    @pl.loop(1, n + 1)
    def _(d):
        peer = lax.rem(me + d, n)
        for g in range(2):
            if wide:
                maps = up[0, g, :, pl.ds(pl.multiple_of(peer * lf, 128), lf)]
            else:
                maps = up[peer, g]
            lora_buf[peer, g] = jnp.dot(
                shrink[:, g * half:(g + 1) * half], maps,
                preferred_element_type=jnp.float32).astype(jnp.bfloat16)

        @pl.when(d < n)
        def _():
            lora_copy(peer, me).start()

    mine = pltpu.make_async_copy(lora_buf.at[me], lora_all.at[me], own_sem.at[3])
    mine.start()

    def landed(block):
        x_copy(xall.at[block], 0, block, lax.rem(me + 1, n)).wait_recv()

    def from_line(step, act, wait):
        @pl.when(z - step >= 0)
        def _():
            block = lax.rem(index(z - step, y, core) + n, n)
            if wait:
                landed(block)
            sends(block, xall.at[block], act, yes, None, True)

        @pl.when(z + step < nz)
        def _():
            block = lax.rem(index(z + step, y, core), n)
            if wait:
                landed(block)
            sends(block, xall.at[block], act, None, yes, True)

    def from_side(zz, act, wait):
        block = lax.rem(index(zz, 1 - y, core) + n, n)
        if wait:
            landed(block)
        act(x_copy(xall.at[block], 3, block, index(z, y, 1 - core)))

    def from_sides(step, act, wait):
        @pl.when(z - step >= 0)
        def _():
            from_side(z - step, act, wait)

        @pl.when(z + step < nz)
        def _():
            from_side(z + step, act, wait)

    @pl.loop(1, nz)
    def _(step):
        from_line(step, begin, True)
        if ny == 2:
            @pl.when(step == 1)
            def _():
                from_side(z, begin, True)

            @pl.when(step > 1)
            def _():
                from_sides(step - 1, begin, True)

    if ny == 2:
        from_sides(nz - 1, begin, True)

    @pl.loop(0, n // 2)
    def _(pair):
        landed(pair * 2 + 1 - core)

    @pl.loop(1, n)
    def _(d):
        peer = lax.rem(me + d, n)
        lora_copy(peer, peer).wait_recv()
        ssq_copy(peer, peer).wait_recv()
        lora_copy(peer, me).wait_send()
        ssq_copy(peer, me).wait_send()
        sp_copy(peer, me).wait_send()

    def finish(copy):
        copy.wait_send()

    sends(me, xg, finish, yes, yes, True)
    if ny == 2:
        from_side(z, finish, False)

    @pl.loop(1, nz)
    def _(step):
        from_line(step, finish, False)
        if ny == 2:
            from_sides(step, finish, False)

    own[1].wait()
    own[2].wait()
    mine.wait()


def project(n, x, w, back, lora, rstd, out, acc):
    k = pl.program_id(0)

    @pl.when(k == 0)
    def _():
        for g in range(2):
            rows = lora[:, g].reshape(lora.shape[0] * lora.shape[2], lora.shape[3])
            acc[g] = 2.0 * jnp.dot(back[...], rows, preferred_element_type=jnp.float32)

    for g in range(2):
        acc[g] += jnp.dot(x[0], w[g], preferred_element_type=jnp.float32)

    @pl.when(k == n - 1)
    def _():
        gate = acc[0] * rstd[...]
        upper = acc[1] * rstd[...]
        out[...] = (gate / (1.0 + jnp.exp(-gate)) * upper).astype(out.dtype)


def per_device(n, x, gain, weight, down, up, row_ids, slots):
    steps, rows, width = x.shape
    lf = weight.shape[2]
    total = steps * rows
    adapters, paired = down.shape[1], down.shape[2]
    rank = paired // 2
    block = steps * CAP
    ny = 2 if n == 16 else 1
    flat = x.reshape(total, width).astype(jnp.float32)
    xg = (flat * gain.astype(jnp.float32)[None, :]).astype(jnp.bfloat16)
    ssq = jnp.sum(flat * flat, axis=1).reshape(total // 128, 128)
    ssq = jnp.pad(ssq, ((0, 8 - total // 128), (0, 0)))

    ids = row_ids.reshape(steps, rows)
    earlier = jnp.arange(rows)[None, :] < jnp.arange(rows)[:, None]
    same = jnp.logical_and(ids[:, :, None] == ids[:, None, :], earlier[None])
    place = jnp.sum(same.astype(jnp.int32), axis=2) + CAP * jnp.arange(steps, dtype=jnp.int32)[:, None]
    place = place.reshape(total)
    ids = ids.reshape(total)
    hot = ids[:, None] == jnp.arange(adapters, dtype=jnp.int32)[None, :]
    slot = jnp.sum(jnp.where(hot, slots[None, :], 0), axis=1)
    spots = jnp.arange(adapters * block, dtype=jnp.int32)
    out_map = (spots[:, None] == (ids * block + place)[None, :]).astype(jnp.bfloat16)
    back = ((slot * block + place)[:, None] == spots[None, :]).astype(jnp.bfloat16)
    sent = jnp.dot(out_map, xg, preferred_element_type=jnp.float32).astype(jnp.bfloat16)
    sp = jnp.einsum("apk,kac->apc", sent.reshape(adapters, block, width), down,
                    preferred_element_type=jnp.float32)
    order = (jnp.arange(adapters, dtype=jnp.int32)[:, None] == slots[None, :]).astype(jnp.float32)
    sp = jnp.einsum("ta,apc->tpc", order, sp, precision=lax.Precision.HIGHEST)

    wide = lf % 128 == 0
    maps = up if wide else up.reshape(2, rank, n, lf).transpose(2, 0, 1, 3)
    vmem = pl.BlockSpec(memory_space=pltpu.VMEM)
    hbm = pl.BlockSpec(memory_space=pl.ANY)
    dma = pltpu.SemaphoreType.DMA
    xall, ssq_all, lora = pl.pallas_call(
        functools.partial(exchange, n, ny, lf, wide),
        out_shape=(
            jax.ShapeDtypeStruct((n, total, width), jnp.bfloat16),
            jax.ShapeDtypeStruct((n, 8, 128), jnp.float32),
            jax.ShapeDtypeStruct((n, 2, block, lf), jnp.bfloat16),
        ),
        in_specs=[vmem] * 4,
        out_specs=(hbm, vmem, vmem),
        scratch_shapes=[
            pltpu.VMEM((n, block, paired), jnp.float32),
            pltpu.VMEM((n, 2, block, lf), jnp.bfloat16),
            dma((4, n)), dma((n,)), dma((n,)), dma((n,)), dma((n,)), dma((n,)),
            dma((n,)), dma((n,)), dma((4,)),
        ],
        compiler_params=pltpu.CompilerParams(
            collective_id=0, has_side_effects=True, vmem_limit_bytes=40 * 2**20),
    )(xg, ssq, sp, maps)
    sums = jnp.sum(ssq_all, axis=0)[: total // 128].reshape(total, 1)
    rstd = lax.rsqrt(sums / (width * n) + 1e-05)
    apart = weight.transpose(1, 0, 2)
    out = pl.pallas_call(
        functools.partial(project, n),
        grid=(n,),
        out_shape=jax.ShapeDtypeStruct((total, lf), jnp.bfloat16),
        in_specs=[
            pl.BlockSpec((1, total, width), lambda k: (k, 0, 0)),
            pl.BlockSpec((2, width, lf), lambda k: (0, k, 0)),
            vmem, vmem, vmem,
        ],
        out_specs=pl.BlockSpec((total, lf), lambda k: (0, 0)),
        scratch_shapes=[pltpu.VMEM((2, total, lf), jnp.float32)],
        compiler_params=pltpu.CompilerParams(vmem_limit_bytes=48 * 2**20),
    )(xall, apart, back, lora, rstd)
    return out.reshape(steps, rows, lf)


def solution(mesh):
    return jax.shard_map(
        functools.partial(per_device, mesh.shape["tensor"]),
        mesh=mesh,
        in_specs=(
            P(None, "groups", "tensor"),
            P("tensor"),
            P(None, None, "tensor"),
            P("tensor", None, None),
            P("tensor", None, None, None),
            P(None, "groups", None),
            P(),
        ),
        out_specs=P(None, "groups", "tensor"),
        check_vma=False,
    )
```

time: 379 us -> 166 us (0.44)
  blocking collectives: 188 us -> 0 us
  Pallas kernels: 0 us -> 134 us
  local copies, waits for them, and re-layouts: 124 us -> 24.6 us
  matrix products: 25.1 us -> 1.58 us
  between operations: 13.5 us -> 0.11 us
  other arithmetic: 17.7 us -> 5.19 us
  starting transfers between devices: 7.58 us -> 0 us
    pallas_call x0 -> x2, Pallas kernels: none -> 134 us  [the longest x1 106 us: per_device(): pl.pallas_call(functools.partial(exchange, n, ny, lf, wide), out_shape=(j...]
    all_gather x1 -> x0, blocking collectives: 109 us -> none  [per_device(): lax.all_gather(gain, 'tensor', axis=0, tiled=True)]
    psum x1 -> x0, blocking collectives: 78.4 us -> none  [per_device(): shrink_output = lax.psum(partial_sum, 'tensor').astype(jnp.bfloat16)]
    dot_general x3 -> x1, local copies, waits for them, and re-layouts: 42.1 us -> 0.09 us  [per_device(): sp = jnp.einsum('ta,apc->tpc', order, sp, precision=lax.Precision.HIGHEST)]
    unnamed x16 -> x15, local copies, waits for them, and re-layouts: 65.7 us -> 24.3 us
    dot_general x4 -> x3, matrix products: 25.1 us -> 1.58 us  [the longest x1 0.73 us: per_device(): jnp.einsum('apk,kac->apc', sent.reshape(adapters, block, width), down, pr...]
    all_to_all x1 -> x0, local copies, waits for them, and re-layouts: 12.1 us -> none  [per_device(): lax.all_to_all(adapter_up_maps, 'tensor', split_axis=3, concat_axis=0, ti...]
    convert_element_type x6 -> x3, other arithmetic: 11.9 us -> 2.11 us  [the longest x2 1.96 us: per_device(): xg = (flat * gain.astype(jnp.float32)[None, :]).astype(jnp.bfloat16)]
  transfers between devices with their start and end apart: 2 -> 0, of which waited for: 0 -> 0; matrix products, arithmetic and copies ran while one was open for 33% -> 0% of each run, Pallas kernels for 0% -> 0%
where the time goes in v1:
time: 166 us; the launch traced here: 165 us
  Pallas kernels  134 us (81%)
  local copies, waits for them, and re-layouts  24.6 us (15%)
  other arithmetic  5.19 us (3%)
    pallas_call x1, Pallas kernels, per_device(): pl.pallas_call(functools.partial(exchange, n, ny, lf, wide), out_shape=(j...  106 us
    pallas_call x1, Pallas kernels, per_device(): pl.pallas_call(functools.partial(project, n), grid=(n,), out_shape=jax.Sh...  28.1 us
    unnamed x15, local copies, waits for them, and re-layouts  24.3 us

profile of v1, /device:TPU:0, one launch (start us, length us, event | category | flops | bytes accessed | tf_op | source)
XLA Modules:
  0.0 165.1 jit_solution(15206144737849122675)
XLA Ops:
  0.0 0.0 copy-start
  0.0 0.8 convert_element_type.30
  0.8 1.2 multiply_reduce_fusion
  2.1 0.8 select_reduce_fusion
  2.9 0.7 copy.27
  3.6 0.2 convert_reduce_fusion
  3.8 0.1 add_bitcast_fusion
  3.9 0.7 multiply_add_fusion
  4.6 1.1 fusion.2.xg
  5.7 0.0 copy-start.5
  5.7 0.4 convolution_convert_fusion
  6.2 0.0 copy-done
  6.2 0.0 copy-start.2
  6.2 0.7 fusion
  7.0 0.4 fusion.5
  7.4 0.1 copy.15.sp
  7.5 0.2 fusion.3.back
  7.6 0.6 copy-done.2
  8.3 105.5 %shard_map.73 = (bf16[16,512,512]{2,1,0:T(8,128)(2,1)}, f32[16,8,128]{2,1,0:T(8,128)S(1)}, bf16[16,2,32,896]{3,2,1,0:T(8,128)(2,1)S(1)}) custom-call(bf16[512,512]{1,0:T(8,128)(2,1)S(1)} %fusion.2.xg, f32[8,128]{1,0:T(8,128)S(1)} %pad.4.ssq, f32[16,32,128]{2,1,0:T(8,128)S(1)} %copy.15.sp, bf16[1,2,64,14336]{3,2,1,0:T(8,128)(2,1)S(1)} %copy-done.2), custom_call_target="tpu_custom_call" | custom-call | tf_op jit(solution)/shard_map/pallas_call | solution.py:246
  113.8 1.2 copy-done.3
  115.1 0.2 copy.17.rstd
  115.2 20.3 %copy.26 = bf16[8192,2,896]{2,0,1:T(8,128)(2,1)} copy(bf16[8192,2,896]{2,1,0:T(2,128)(2,1)} %param.9) | data formatting | bytes 58720256 | tf_op args[2]
  135.5 1.5 copy-done.4
  137.0 28.1 %shard_map.74 = bf16[512,896]{1,0:T(8,128)(2,1)} custom-call(bf16[16,512,512]{2,1,0:T(8,128)(2,1)} %get-tuple-element.8.x, bf16[2,8192,896]{2,1,0:T(8,128)(2,1)} %bitcast.22, bf16[512,512]{1,0:T(8,128)(2,1)S(1)} %fusion.3.back, bf16[16,2,32,896]{3,2,1,0:T(8,128)(2,1)S(1)} %copy-done.4, f32[512,1]{1,0:T(8,128)S(1)} %copy.17.rstd), custom_call_target="tpu_custom_call" | custom-call | tf_op jit(solution)/shard_map/pallas_call | solution.py:267
  (12 shorter events, 0.1 us)
Async XLA Ops:
  0.0 6.2 %copy-start = (bf16[512,16,128]{2,1,0:T(8,128)(2,1)S(1)}, bf16[512,16,128]{2,1,0:T(8,128)(2,1)}, u32[]{:S(2)}) copy-start(bf16[512,16,128]{2,1,0:T(8,128)(2,1)} %param.10) | copy-start | bytes 6291460
  5.7 1.2 copy-start.5
  6.2 2.0 %copy-start.2 = (bf16[1,2,64,14336]{3,2,1,0:T(8,128)(2,1)S(1)}, bf16[1,2,64,14336]{3,2,1,0:T(8,128)(2,1)}, u32[]{:S(2)}) copy-start(bf16[1,2,64,14336]{3,2,1,0:T(8,128)(2,1)} %up.1) | copy-start | bytes 11010052
  113.8 1.2 copy-start.3
  135.5 1.5 copy-start.4
  137.0 28.1 %copy-start.1 = (bf16[512,16,128]{2,1,0:T(8,128)(2,1)S(1)}, bf16[512,16,128]{2,1,0:T(8,128)(2,1)}, u32[]{:S(2)}) copy-start(bf16[512,16,128]{2,1,0:T(8,128)(2,1)} %param.10) | copy-start | bytes 6291460

commit v2 on v1

v2 whole, which is shorter than its diff:
```python
import functools
import jax
import jax.numpy as jnp
from jax import lax
from jax.experimental import pallas as pl
from jax.experimental.pallas import tpu as pltpu
from jax.sharding import PartitionSpec as P

CAP = 16
MESH = pl.DeviceIdType.MESH


def exchange(n, ny, lf, wide, xg, ssq, sp, up, back, weight, out, xall, ssq_all,
             lora_all, sp_all, lora_buf, w, acc, x_send, x_recv, q_send, q_recv,
             s_send, s_recv, l_send, l_recv, own_sem):
    nz = n // (2 * ny)
    me = lax.axis_index("tensor")
    core = lax.rem(me, 2)
    y = lax.rem(me // 2, ny)
    z = me // (2 * ny)
    half = up.shape[-2]
    total, width = xg.shape
    part = total // 2

    def index(zz, yy, cc):
        return lax.rem((zz * ny + yy) * 2 + cc + n, n)

    load = pltpu.make_async_copy(weight, w, own_sem.at[2])
    load.start()

    barrier = pltpu.get_barrier_semaphore()

    @pl.loop(1, n)
    def _(d):
        pl.semaphore_signal(barrier, inc=1, device_id={"tensor": lax.rem(me + d, n)},
                            device_id_type=MESH)

    pl.semaphore_wait(barrier, n - 1)

    def remote(src, dst, send, recv, peer):
        return pltpu.make_async_remote_copy(
            src_ref=src, dst_ref=dst, send_sem=send, recv_sem=recv,
            device_id={"tensor": peer}, device_id_type=MESH)

    def sp_copy(peer, slot):
        return remote(sp.at[peer], sp_all.at[slot], s_send.at[peer], s_recv.at[slot], peer)

    def ssq_copy(peer, slot):
        return remote(ssq, ssq_all.at[slot], q_send.at[peer], q_recv.at[slot], peer)

    def lora_copy(peer, slot):
        return remote(lora_buf.at[peer], lora_all.at[slot], l_send.at[peer],
                      l_recv.at[slot], peer)

    def rows(h):
        return pl.ds(h * part, part)

    def x_copy(own, way, block, h, peer):
        src = xg.at[rows(h)] if own else xall.at[block, rows(h)]
        return remote(src, xall.at[block, rows(h)], x_send.at[way, block, h],
                      x_recv.at[block, h], peer)

    def sends(block, h, own, act, rising, falling, across):
        if rising:
            @pl.when(z + 1 < nz)
            def _():
                act(x_copy(own, 0, block, h, index(z + 1, y, core)))
        if falling:
            @pl.when(z > 0)
            def _():
                act(x_copy(own, 1, block, h, index(z - 1, y, core)))
        if across and ny == 2:
            act(x_copy(own, 2, block, h, index(z, 1 - y, core)))
        act(x_copy(own, 3, block, h, index(z, y, 1 - core)))

    def landed(block, h):
        x_copy(False, 0, block, h, lax.rem(me + 1, n)).wait_recv()

    def both(step, run):
        @pl.when(jnp.logical_and(step >= 0, z - step >= 0))
        def _():
            run(z - step, True)

        @pl.when(jnp.logical_and(step > 0, z + step < nz))
        def _():
            run(z + step, False)

    def relay(step, act, wait):
        for h in range(2):
            def line(zz, rising):
                block = index(zz, y, core)
                if wait:
                    landed(block, h)
                sends(block, h, False, act, rising, not rising, True)

            both(step, line)

    def relay_side(step, act, wait):
        for h in range(2):
            def side(zz, rising):
                block = index(zz, 1 - y, core)
                if wait:
                    landed(block, h)
                act(x_copy(False, 3, block, h, index(z, y, 1 - core)))

            both(step, side)

    def use(step, yy, cc, wait):
        def one(zz, rising):
            block = index(zz, yy, cc)
            if wait:
                landed(block, 0)
                landed(block, 1)
            for g in range(2):
                acc[g] += jnp.dot(xall[block], w[g, pl.ds(pl.multiple_of(block * width, 128), width)],
                                  preferred_element_type=jnp.float32)

        both(step, one)

    def begin(copy):
        copy.start()

    def finish(copy):
        copy.wait_send()

    @pl.loop(1, n)
    def _(d):
        sp_copy(lax.rem(me + d, n), me).start()

    for h in range(2):
        sends(me, h, True, begin, True, True, True)

    @pl.loop(1, n)
    def _(d):
        ssq_copy(lax.rem(me + d, n), me).start()

    own = [pltpu.make_async_copy(sp.at[me], sp_all.at[me], own_sem.at[0]),
           pltpu.make_async_copy(ssq, ssq_all.at[me], own_sem.at[1])]
    for copy in own:
        copy.start()
    own[0].wait()

    @pl.loop(1, n)
    def _(d):
        peer = lax.rem(me + d, n)
        sp_copy(peer, peer).wait_recv()

    shrink = jnp.sum(sp_all[...], axis=0).astype(jnp.bfloat16)

    @pl.loop(1, n + 1)
    def _(d):
        peer = lax.rem(me + d, n)
        for g in range(2):
            if wide:
                maps = up[0, g, :, pl.ds(pl.multiple_of(peer * lf, 128), lf)]
            else:
                maps = up[peer, g]
            lora_buf[peer, g] = jnp.dot(
                shrink[:, g * half:(g + 1) * half], maps,
                preferred_element_type=jnp.float32).astype(jnp.bfloat16)

        @pl.when(d < n)
        def _():
            lora_copy(peer, me).start()

    mine = pltpu.make_async_copy(lora_buf.at[me], lora_all.at[me], own_sem.at[3])
    mine.start()

    load.wait()
    for g in range(2):
        acc[g] = jnp.dot(xg[...], w[g, pl.ds(pl.multiple_of(me * width, 128), width)],
                         preferred_element_type=jnp.float32)

    @pl.loop(1, nz)
    def _(step):
        relay(step, begin, True)
        if ny == 2:
            relay_side(step - 1, begin, True)
        use(step, y, core, False)
        use(step - 1, y, 1 - core, True)
        if ny == 2:
            use(step - 1, 1 - y, core, False)
            use(step - 2, 1 - y, 1 - core, True)

    if ny == 2:
        relay_side(nz - 1, begin, True)
        use(nz - 1, 1 - y, core, False)
        use(nz - 2, 1 - y, 1 - core, True)
    use(nz - 1, y, 1 - core, True)

    @pl.loop(1, n)
    def _(d):
        peer = lax.rem(me + d, n)
        lora_copy(peer, peer).wait_recv()
        ssq_copy(peer, peer).wait_recv()

    own[1].wait()
    mine.wait()
    for g in range(2):
        flat = lora_all[:, g].reshape(back.shape[1], lf)
        acc[g] += 2.0 * jnp.dot(back[...], flat, preferred_element_type=jnp.float32)
    if ny == 2:
        use(nz - 1, 1 - y, 1 - core, True)

    sums = jnp.sum(ssq_all[...], axis=0)
    diagonal = (lax.broadcasted_iota(jnp.int32, (128, 128), 0)
                == lax.broadcasted_iota(jnp.int32, (128, 128), 1))
    for i in range(total // 128):
        line = jnp.broadcast_to(sums[i:i + 1, :], (128, 128))
        column = jnp.sum(jnp.where(diagonal, line, 0.0), axis=1, keepdims=True)
        rstd = lax.rsqrt(column / (width * n) + 1e-05)
        gate = acc[0, i * 128:(i + 1) * 128] * rstd
        upper = acc[1, i * 128:(i + 1) * 128] * rstd
        out[i * 128:(i + 1) * 128, :] = (
            gate / (1.0 + jnp.exp(-gate)) * upper).astype(out.dtype)

    @pl.loop(1, n)
    def _(d):
        peer = lax.rem(me + d, n)
        lora_copy(peer, me).wait_send()
        ssq_copy(peer, me).wait_send()
        sp_copy(peer, me).wait_send()

    for h in range(2):
        sends(me, h, True, finish, True, True, True)

    @pl.loop(1, nz)
    def _(step):
        relay(step, finish, False)

    if ny == 2:
        @pl.loop(0, nz)
        def _(step):
            relay_side(step, finish, False)


def per_device(n, x, gain, weight, down, up, row_ids, slots):
    steps, rows, width = x.shape
    lf = weight.shape[2]
    total = steps * rows
    adapters, paired = down.shape[1], down.shape[2]
    rank = paired // 2
    block = steps * CAP
    ny = 2 if n == 16 else 1
    flat = x.reshape(total, width).astype(jnp.float32)
    xg = (flat * gain.astype(jnp.float32)[None, :]).astype(jnp.bfloat16)
    ssq = jnp.sum(flat * flat, axis=1).reshape(total // 128, 128)
    ssq = jnp.pad(ssq, ((0, 8 - total // 128), (0, 0)))

    ids = row_ids.reshape(steps, rows)
    earlier = jnp.arange(rows)[None, :] < jnp.arange(rows)[:, None]
    same = jnp.logical_and(ids[:, :, None] == ids[:, None, :], earlier[None])
    place = jnp.sum(same.astype(jnp.int32), axis=2) + CAP * jnp.arange(steps, dtype=jnp.int32)[:, None]
    place = place.reshape(total)
    ids = ids.reshape(total)
    hot = ids[:, None] == jnp.arange(adapters, dtype=jnp.int32)[None, :]
    slot = jnp.sum(jnp.where(hot, slots[None, :], 0), axis=1)
    spots = jnp.arange(adapters * block, dtype=jnp.int32)
    out_map = (spots[:, None] == (ids * block + place)[None, :]).astype(jnp.bfloat16)
    back = ((slot * block + place)[:, None] == spots[None, :]).astype(jnp.bfloat16)
    sent = jnp.dot(out_map, xg, preferred_element_type=jnp.float32).astype(jnp.bfloat16)
    sp = jnp.einsum("apk,kac->apc", sent.reshape(adapters, block, width), down,
                    preferred_element_type=jnp.float32)
    order = (jnp.arange(adapters, dtype=jnp.int32)[:, None] == slots[None, :]).astype(jnp.float32)
    sp = jnp.einsum("ta,apc->tpc", order, sp, precision=lax.Precision.HIGHEST)

    wide = lf % 128 == 0
    maps = up if wide else up.reshape(2, rank, n, lf).transpose(2, 0, 1, 3)
    vmem = pl.BlockSpec(memory_space=pltpu.VMEM)
    hbm = pl.BlockSpec(memory_space=pl.ANY)
    dma = pltpu.SemaphoreType.DMA
    apart = weight.transpose(1, 0, 2)
    out = pl.pallas_call(
        functools.partial(exchange, n, ny, lf, wide),
        out_shape=jax.ShapeDtypeStruct((total, lf), jnp.bfloat16),
        in_specs=[vmem] * 5 + [hbm],
        out_specs=vmem,
        scratch_shapes=[
            pltpu.VMEM((n, total, width), jnp.bfloat16),
            pltpu.VMEM((n, 8, 128), jnp.float32),
            pltpu.VMEM((n, 2, block, lf), jnp.bfloat16),
            pltpu.VMEM((n, block, paired), jnp.float32),
            pltpu.VMEM((n, 2, block, lf), jnp.bfloat16),
            pltpu.VMEM((2, n * width, lf), jnp.bfloat16),
            pltpu.VMEM((2, total, lf), jnp.float32),
            dma((4, n, 2)), dma((n, 2)), dma((n,)), dma((n,)), dma((n,)), dma((n,)),
            dma((n,)), dma((n,)), dma((4,)),
        ],
        compiler_params=pltpu.CompilerParams(
            collective_id=0, has_side_effects=True, vmem_limit_bytes=60 * 2**20),
    )(xg, ssq, sp, maps, back, apart)
    return out.reshape(steps, rows, lf)


def solution(mesh):
    return jax.shard_map(
        functools.partial(per_device, mesh.shape["tensor"]),
        mesh=mesh,
        in_specs=(
            P(None, "groups", "tensor"),
            P("tensor"),
            P(None, None, "tensor"),
            P("tensor", None, None),
            P("tensor", None, None, None),
            P(None, "groups", None),
            P(),
        ),
        out_specs=P(None, "groups", "tensor"),
        check_vma=False,
    )
```

time: 166 us -> 136 us (0.82)
  Pallas kernels: 134 us -> 104 us
    pallas_call x2 -> x1, Pallas kernels: 134 us -> 104 us  [per_device(): pl.pallas_call(functools.partial(exchange, n, ny, lf, wide), out_shape=ja...]
    unnamed x15 -> x12, local copies, waits for them, and re-layouts: 24.3 us -> 23.2 us
where the time goes in v2:
time: 136 us
  Pallas kernels  104 us (76%)
  local copies, waits for them, and re-layouts  24.6 us (18%)
  other arithmetic  5.94 us (4%)
  matrix products  1.57 us (1%)
    pallas_call x1, Pallas kernels, per_device(): pl.pallas_call(functools.partial(exchange, n, ny, lf, wide), out_shape=ja...  104 us
    unnamed x12, local copies, waits for them, and re-layouts  23.2 us

profile of v2, /device:TPU:0, one launch (start us, length us, event | category | flops | bytes accessed | tf_op | source)
XLA Modules:
  0.0 136.0 jit_solution(382766588922235534)
XLA Ops:
  0.0 0.0 copy-start
  0.0 0.8 convert_element_type.30
  0.8 1.2 multiply_reduce_fusion
  2.1 0.6 pad.4.ssq
  2.7 0.8 select_reduce_fusion
  3.5 0.7 copy.23
  4.2 0.2 convert_reduce_fusion
  4.4 0.1 add_bitcast_fusion
  4.5 0.7 multiply_add_fusion
  5.2 1.1 fusion.2.xg
  6.3 0.0 copy-start.2
  6.3 0.0 copy-start.3
  6.4 0.4 convolution_convert_fusion
  6.8 0.0 copy-done
  6.8 0.7 fusion
  7.5 0.0 copy-done.2
  7.6 0.0 copy-done.3
  7.6 0.4 fusion.5
  8.0 0.8 copy.11.sp
  8.8 0.9 fusion.3.back
  9.7 20.3 %copy.22 = bf16[8192,2,896]{2,0,1:T(8,128)(2,1)} copy(bf16[8192,2,896]{2,1,0:T(2,128)(2,1)} %param.9) | data formatting | bytes 58720256 | tf_op args[2]
  30.0 103.7 %shard_map.73 = bf16[512,896]{1,0:T(8,128)(2,1)} custom-call(bf16[512,512]{1,0:T(8,128)(2,1)} %copy-done.2, f32[8,128]{1,0:T(8,128)} %pad.4.ssq, f32[16,32,128]{2,1,0:T(8,128)} %copy.11.sp, bf16[1,2,64,14336]{3,2,1,0:T(8,128)(2,1)} %up.1, bf16[512,512]{1,0:T(8,128)(2,1)} %fusion.3.back, bf16[2,8192,896]{2,1,0:T(8,128)(2,1)} %bitcast.21), custom_call_target="tpu_custom_call" | custom-call | tf_op jit(solution)/shard_map/pallas_call | solution.py:273
  133.8 2.2 %copy.25 = bf16[2,256,896]{2,1,0:T(8,128)(2,1)} copy(bf16[2,256,896]{2,1,0:T(8,128)(2,1)} %bitcast.22) | data formatting | bytes 1835008
  136.0 0.0 copy-done.1
  (5 shorter events, 0.1 us)
Async XLA Ops:
  0.0 6.8 %copy-start = (bf16[512,16,128]{2,1,0:T(8,128)(2,1)S(1)}, bf16[512,16,128]{2,1,0:T(8,128)(2,1)}, u32[]{:S(2)}) copy-start(bf16[512,16,128]{2,1,0:T(8,128)(2,1)} %param.10) | copy-start | bytes 6291460
  6.3 1.2 copy-start.2
  6.3 1.2 copy-start.3
  30.0 105.9 %copy-start.1 = (bf16[512,16,128]{2,1,0:T(8,128)(2,1)S(1)}, bf16[512,16,128]{2,1,0:T(8,128)(2,1)}, u32[]{:S(2)}) copy-start(bf16[512,16,128]{2,1,0:T(8,128)(2,1)} %param.10) | copy-start | bytes 6291460

commit v3 on v2

--- a/solution.py
+++ b/solution.py
@@ -10,7 +10,8 @@
 MESH = pl.DeviceIdType.MESH
 
 
-def exchange(n, ny, lf, wide, xg, ssq, sp, up, back, weight, out, xall, ssq_all,
+def exchange(n, ny, lf, wide, xg, ssq, sp, up, back, weight, below, above,
+             aside, beside, out, xall, ssq_all,
              lora_all, sp_all, lora_buf, w, acc, x_send, x_recv, q_send, q_recv,
              s_send, s_recv, l_send, l_recv, own_sem):
     nz = n // (2 * ny)
@@ -28,6 +29,21 @@
     load = pltpu.make_async_copy(weight, w, own_sem.at[2])
     load.start()
 
+    def placed(act):
+        if nz > 1:
+            @pl.when(z > 0)
+            def _():
+                act(pltpu.make_async_copy(below, xall.at[index(z - 1, y, core)], own_sem.at[4]))
+
+            @pl.when(z + 1 < nz)
+            def _():
+                act(pltpu.make_async_copy(above, xall.at[index(z + 1, y, core)], own_sem.at[5]))
+        if ny == 2:
+            act(pltpu.make_async_copy(aside, xall.at[index(z, 1 - y, core)], own_sem.at[6]))
+        act(pltpu.make_async_copy(beside, xall.at[index(z, y, 1 - core)], own_sem.at[7]))
+
+    placed(lambda copy: copy.start())
+
     barrier = pltpu.get_barrier_semaphore()
 
     @pl.loop(1, n)
@@ -55,29 +71,28 @@
     def rows(h):
         return pl.ds(h * part, part)
 
-    def x_copy(own, way, block, h, peer):
-        src = xg.at[rows(h)] if own else xall.at[block, rows(h)]
-        return remote(src, xall.at[block, rows(h)], x_send.at[way, block, h],
+    def x_copy(way, block, h, peer):
+        return remote(xall.at[block, rows(h)], xall.at[block, rows(h)], x_send.at[way, block, h],
                       x_recv.at[block, h], peer)
 
-    def sends(block, h, own, act, rising, falling, across):
+    def sends(block, h, act, rising):
         if rising:
             @pl.when(z + 1 < nz)
             def _():
-                act(x_copy(own, 0, block, h, index(z + 1, y, core)))
-        if falling:
+                act(x_copy(0, block, h, index(z + 1, y, core)))
+        else:
             @pl.when(z > 0)
             def _():
-                act(x_copy(own, 1, block, h, index(z - 1, y, core)))
-        if across and ny == 2:
-            act(x_copy(own, 2, block, h, index(z, 1 - y, core)))
-        act(x_copy(own, 3, block, h, index(z, y, 1 - core)))
+                act(x_copy(1, block, h, index(z - 1, y, core)))
+        if ny == 2:
+            act(x_copy(2, block, h, index(z, 1 - y, core)))
+        act(x_copy(3, block, h, index(z, y, 1 - core)))
 
     def landed(block, h):
-        x_copy(False, 0, block, h, lax.rem(me + 1, n)).wait_recv()
+        x_copy(0, block, h, lax.rem(me + 1, n)).wait_recv()
 
     def both(step, run):
-        @pl.when(jnp.logical_and(step >= 0, z - step >= 0))
+        @pl.when(z - step >= 0)
         def _():
             run(z - step, True)
 
@@ -91,7 +106,7 @@
                 block = index(zz, y, core)
                 if wait:
                     landed(block, h)
-                sends(block, h, False, act, rising, not rising, True)
+                sends(block, h, act, rising)
 
             both(step, line)
 
@@ -101,7 +116,7 @@
                 block = index(zz, 1 - y, core)
                 if wait:
                     landed(block, h)
-                act(x_copy(False, 3, block, h, index(z, y, 1 - core)))
+                act(x_copy(3, block, h, index(z, y, 1 - core)))
 
             both(step, side)
 
@@ -127,8 +142,10 @@
     def _(d):
         sp_copy(lax.rem(me + d, n), me).start()
 
-    for h in range(2):
-        sends(me, h, True, begin, True, True, True)
+    placed(lambda copy: copy.wait())
+    relay(1, begin, False)
+    if ny == 2:
+        relay_side(0, begin, False)
 
     @pl.loop(1, n)
     def _(d):
@@ -171,7 +188,12 @@
         acc[g] = jnp.dot(xg[...], w[g, pl.ds(pl.multiple_of(me * width, 128), width)],
                          preferred_element_type=jnp.float32)
 
-    @pl.loop(1, nz)
+    use(1, y, core, False)
+    use(0, y, 1 - core, False)
+    if ny == 2:
+        use(0, 1 - y, core, False)
+
+    @pl.loop(2, nz)
     def _(step):
         relay(step, begin, True)
         if ny == 2:
@@ -220,9 +242,6 @@
         lora_copy(peer, me).wait_send()
         ssq_copy(peer, me).wait_send()
         sp_copy(peer, me).wait_send()
-
-    for h in range(2):
-        sends(me, h, True, finish, True, True, True)
 
     @pl.loop(1, nz)
     def _(step):
@@ -246,6 +265,13 @@
     xg = (flat * gain.astype(jnp.float32)[None, :]).astype(jnp.bfloat16)
     ssq = jnp.sum(flat * flat, axis=1).reshape(total // 128, 128)
     ssq = jnp.pad(ssq, ((0, 8 - total // 128), (0, 0)))
+
+    stride = 2 * ny
+    pairs = [[(i, i + stride) for i in range(n - stride)],
+             [(i + stride, i) for i in range(n - stride)],
+             [(i, i ^ 2 if ny == 2 else i ^ 1) for i in range(n)],
+             [(i, i ^ 1) for i in range(n)]]
+    near = [lax.ppermute(xg, "tensor", perm) for perm in pairs]
 
     ids = row_ids.reshape(steps, rows)
     earlier = jnp.arange(rows)[None, :] < jnp.arange(rows)[:, None]
@@ -273,7 +299,7 @@
     out = pl.pallas_call(
         functools.partial(exchange, n, ny, lf, wide),
         out_shape=jax.ShapeDtypeStruct((total, lf), jnp.bfloat16),
-        in_specs=[vmem] * 5 + [hbm],
+        in_specs=[vmem] * 5 + [hbm] * 5,
         out_specs=vmem,
         scratch_shapes=[
             pltpu.VMEM((n, total, width), jnp.bfloat16),
@@ -284,11 +310,11 @@
             pltpu.VMEM((2, n * width, lf), jnp.bfloat16),
             pltpu.VMEM((2, total, lf), jnp.float32),
             dma((4, n, 2)), dma((n, 2)), dma((n,)), dma((n,)), dma((n,)), dma((n,)),
-            dma((n,)), dma((n,)), dma((4,)),
+            dma((n,)), dma((n,)), dma((8,)),
         ],
         compiler_params=pltpu.CompilerParams(
             collective_id=0, has_side_effects=True, vmem_limit_bytes=60 * 2**20),
-    )(xg, ssq, sp, maps, back, apart)
+    )(xg, ssq, sp, maps, back, apart, *near)
     return out.reshape(steps, rows, lf)
 
 

time: 136 us -> 126 us (0.926)
  Pallas kernels: 104 us -> 84 us
  starting transfers between devices: 0 us -> 9.74 us
    pallas_call x1, Pallas kernels: 104 us -> 84 us  [per_device(): pl.pallas_call(functools.partial(exchange, n, ny, lf, wide), out_shape=ja...]
    ppermute x0 -> x4, starting transfers between devices: none -> 9.74 us  [per_device(): near = [lax.ppermute(xg, 'tensor', perm) for perm in pairs]]
    unnamed x12 -> x16, local copies, waits for them, and re-layouts: 23.2 us -> 23.6 us
  transfers between devices with their start and end apart: 0 -> 4, of which waited for: 0 -> 0; matrix products, arithmetic and copies ran while one was open for 0% -> 21% of each run, Pallas kernels for 0% -> 0%
where the time goes in v3:
time: 126 us; the launch traced here: 125 us
  Pallas kernels  84 us (67%)
  local copies, waits for them, and re-layouts  25 us (20%)
  starting transfers between devices  9.74 us (8%)
  other arithmetic  4.91 us (4%)
  matrix products  1.58 us (1%)
    pallas_call x1, Pallas kernels, per_device(): pl.pallas_call(functools.partial(exchange, n, ny, lf, wide), out_shape=ja...  84 us
    unnamed x16, local copies, waits for them, and re-layouts  23.6 us
    ppermute x4, starting transfers between devices, per_device(): near = [lax.ppermute(xg, 'tensor', perm) for perm in pairs]  9.74 us
  transfers between devices with their start and end apart: 4, of which 0 were waited for; matrix products, arithmetic and copies ran while one was open for 21% of the time, Pallas kernels for 0%

profile of v3, /device:TPU:0, one launch (start us, length us, event | category | flops | bytes accessed | tf_op | source)
XLA Modules:
  0.0 125.4 jit_solution(1052382749896222585)
XLA Ops:
  0.0 0.8 convert_element_type.30
  0.8 1.1 fusion.2.xg
  2.0 0.0 copy-start.2
  2.0 0.5 collective-permute-start.3
  2.5 2.6 %collective-permute-start.2 = (bf16[512,512]{1,0:T(8,128)(2,1)S(1)}, bf16[512,512]{1,0:T(8,128)(2,1)}, u32[]{:S(2)}, u32[]{:S(2)}) collective-permute-start(bf16[512,512]{1,0:T(8,128)(2,1)S(1)} %fusion.2.xg), channel_id=1, source_target_pairs={{0,2},{1,3},{2,0},{3,1},{4,6},{5,7},{6,4},{7,5},{8,10},{9,11},{10,... | collective-permute-start | bytes 1572872 | tf_op jit(solution)/shard_map/ppermute | solution.py:274
  5.1 1.3 %collective-permute-start.1 = (bf16[512,512]{1,0:T(8,128)(2,1)S(1)}, bf16[512,512]{1,0:T(8,128)(2,1)}, u32[]{:S(2)}, u32[]{:S(2)}) collective-permute-start(bf16[512,512]{1,0:T(8,128)(2,1)S(1)} %fusion.2.xg), channel_id=1, source_target_pairs={{4,0},{5,1},{6,2},{7,3},{8,4},{9,5},{10,6},{11,7},{12,8},{13,9},{1... | collective-permute-start | bytes 1572872 | tf_op jit(solution)/shard_map/ppermute | solution.py:274
  6.4 5.4 %collective-permute-start = (bf16[512,512]{1,0:T(8,128)(2,1)S(1)}, bf16[512,512]{1,0:T(8,128)(2,1)}, u32[]{:S(2)}, u32[]{:S(2)}) collective-permute-start(bf16[512,512]{1,0:T(8,128)(2,1)S(1)} %fusion.2.xg), channel_id=1, source_target_pairs={{0,4},{1,5},{2,6},{3,7},{4,8},{5,9},{6,10},{7,11},{8,12},{9,13},{1... | collective-permute-start | bytes 1572872 | tf_op jit(solution)/shard_map/ppermute | solution.py:274
  11.8 0.7 copy.23
  12.5 0.2 convert_reduce_fusion
  12.7 0.1 add_bitcast_fusion
  12.8 0.8 select_reduce_fusion
  13.6 0.7 multiply_add_fusion
  14.3 0.4 convolution_convert_fusion
  14.7 0.7 fusion
  15.5 0.2 multiply_reduce_fusion
  15.7 0.4 fusion.5
  16.1 0.8 copy.11.sp
  16.9 20.0 %copy.22 = bf16[8192,2,896]{2,0,1:T(8,128)(2,1)} copy(bf16[8192,2,896]{2,1,0:T(2,128)(2,1)} %param.9) | data formatting | bytes 58720256 | tf_op args[2]
  36.9 0.6 pad.4.ssq
  37.5 0.9 fusion.3.back
  38.4 0.0 collective-permute-done.3.beside
  38.4 0.8 copy-done.4
  39.2 84.0 %shard_map.73 = bf16[512,896]{1,0:T(8,128)(2,1)} custom-call(bf16[512,512]{1,0:T(8,128)(2,1)} %copy-done.2, f32[8,128]{1,0:T(8,128)} %pad.4.ssq, f32[16,32,128]{2,1,0:T(8,128)} %copy.11.sp, bf16[1,2,64,14336]{3,2,1,0:T(8,128)(2,1)} %up.1, bf16[512,512]{1,0:T(8,128)(2,1)} %fusion.3.back, bf16[2,8192,896]{2,1,0:T(8,128)(2,1)} %bitcast.21, ...), custom_call_target="tpu_custom_call" | custom-call | tf_op jit(solution)/shard_map/pallas_call | solution.py:299
  123.3 2.2 %copy.25 = bf16[2,256,896]{2,1,0:T(8,128)(2,1)} copy(bf16[2,256,896]{2,1,0:T(8,128)(2,1)} %bitcast.22) | data formatting | bytes 1835008
  (17 shorter events, 0.1 us)
Async XLA Ops:
  0.0 14.7 %copy-start = (bf16[512,16,128]{2,1,0:T(8,128)(2,1)S(1)}, bf16[512,16,128]{2,1,0:T(8,128)(2,1)}, u32[]{:S(2)}) copy-start(bf16[512,16,128]{2,1,0:T(8,128)(2,1)} %param.10) | copy-start | bytes 6291460
  2.0 13.5 %copy-start.2 = (bf16[512,512]{1,0:T(8,128)(2,1)}, bf16[512,512]{1,0:T(8,128)(2,1)S(1)}, u32[]{:S(2)}) copy-start(bf16[512,512]{1,0:T(8,128)(2,1)S(1)} %fusion.2.xg) | copy-start | bytes 1572868
  2.0 36.4 %collective-permute-start.3 = (bf16[512,512]{1,0:T(8,128)(2,1)S(1)}, bf16[512,512]{1,0:T(8,128)(2,1)S(1)}, u32[]{:S(2)}, u32[]{:S(2)}) collective-permute-start(bf16[512,512]{1,0:T(8,128)(2,1)S(1)} %fusion.2.xg), channel_id=1, source_target_pairs={{0,1},{1,0},{2,3},{3,2},{4,5},{5,4},{6,7},{7,6},{8,9},{9,8},{10,11... | collective-permute-start | bytes 1572872 | tf_op jit(solution)/shard_map/ppermute | solution.py:274
  2.5 35.9 %collective-permute-start.2 = (bf16[512,512]{1,0:T(8,128)(2,1)S(1)}, bf16[512,512]{1,0:T(8,128)(2,1)}, u32[]{:S(2)}, u32[]{:S(2)}) collective-permute-start(bf16[512,512]{1,0:T(8,128)(2,1)S(1)} %fusion.2.xg), channel_id=1, source_target_pairs={{0,2},{1,3},{2,0},{3,1},{4,6},{5,7},{6,4},{7,5},{8,10},{9,11},{10,... | collective-permute-start | bytes 1572872 | tf_op jit(solution)/shard_map/ppermute | solution.py:274
  5.1 33.3 %collective-permute-start.1 = (bf16[512,512]{1,0:T(8,128)(2,1)S(1)}, bf16[512,512]{1,0:T(8,128)(2,1)}, u32[]{:S(2)}, u32[]{:S(2)}) collective-permute-start(bf16[512,512]{1,0:T(8,128)(2,1)S(1)} %fusion.2.xg), channel_id=1, source_target_pairs={{4,0},{5,1},{6,2},{7,3},{8,4},{9,5},{10,6},{11,7},{12,8},{13,9},{1... | collective-permute-start | bytes 1572872 | tf_op jit(solution)/shard_map/ppermute | solution.py:274
  6.4 32.0 %collective-permute-start = (bf16[512,512]{1,0:T(8,128)(2,1)S(1)}, bf16[512,512]{1,0:T(8,128)(2,1)}, u32[]{:S(2)}, u32[]{:S(2)}) collective-permute-start(bf16[512,512]{1,0:T(8,128)(2,1)S(1)} %fusion.2.xg), channel_id=1, source_target_pairs={{0,4},{1,5},{2,6},{3,7},{4,8},{5,9},{6,10},{7,11},{8,12},{9,13},{1... | collective-permute-start | bytes 1572872 | tf_op jit(solution)/shard_map/ppermute | solution.py:274
  14.3 1.2 copy-start.3
  14.3 1.4 %copy-start.5 = (s32[16]{0:T(128)S(1)}, s32[16]{0:T(128)}, u32[]{:S(2)}) copy-start(s32[16]{0:T(128)} %param.13) | copy-start | bytes 196
  38.4 0.8 copy-start.4
  39.2 86.2 %copy-start.1 = (bf16[512,16,128]{2,1,0:T(8,128)(2,1)S(1)}, bf16[512,16,128]{2,1,0:T(8,128)(2,1)}, u32[]{:S(2)}) copy-start(bf16[512,16,128]{2,1,0:T(8,128)(2,1)} %param.10) | copy-start | bytes 6291460

commit v4 on v3

--- a/solution.py
+++ b/solution.py
@@ -183,6 +183,10 @@
     mine = pltpu.make_async_copy(lora_buf.at[me], lora_all.at[me], own_sem.at[3])
     mine.start()
 
+    relay(2, begin, True)
+    if ny == 2:
+        relay_side(1, begin, True)
+
     load.wait()
     for g in range(2):
         acc[g] = jnp.dot(xg[...], w[g, pl.ds(pl.multiple_of(me * width, 128), width)],
@@ -193,19 +197,24 @@
     if ny == 2:
         use(0, 1 - y, core, False)
 
-    @pl.loop(2, nz)
+    @pl.loop(3, nz)
     def _(step):
         relay(step, begin, True)
         if ny == 2:
             relay_side(step - 1, begin, True)
-        use(step, y, core, False)
-        use(step - 1, y, 1 - core, True)
+        use(step - 1, y, core, False)
+        use(step - 2, y, 1 - core, True)
         if ny == 2:
-            use(step - 1, 1 - y, core, False)
-            use(step - 2, 1 - y, 1 - core, True)
+            use(step - 2, 1 - y, core, False)
+            use(step - 3, 1 - y, 1 - core, True)
 
     if ny == 2:
         relay_side(nz - 1, begin, True)
+    use(nz - 1, y, core, False)
+    use(nz - 2, y, 1 - core, True)
+    if ny == 2:
+        use(nz - 2, 1 - y, core, False)
+        use(nz - 3, 1 - y, 1 - core, True)
         use(nz - 1, 1 - y, core, False)
         use(nz - 2, 1 - y, 1 - core, True)
     use(nz - 1, y, 1 - core, True)

time: 126 us -> 131 us (1.040)
  Pallas kernels: 84 us -> 89.1 us
    pallas_call x1, Pallas kernels: 84 us -> 89.1 us  [per_device(): pl.pallas_call(functools.partial(exchange, n, ny, lf, wide), out_shape=ja...]
  transfers between devices with their start and end apart: 4 -> 4, of which waited for: 0 -> 0; matrix products, arithmetic and copies ran while one was open for 21% -> 20% of each run, Pallas kernels for 0% -> 0%
where the time goes in v4:
time: 131 us; the launch traced here: 130 us
  Pallas kernels  89.1 us (68%)
  local copies, waits for them, and re-layouts  25 us (19%)
  starting transfers between devices  9.74 us (7%)
  other arithmetic  4.91 us (4%)
  matrix products  1.58 us (1%)
    pallas_call x1, Pallas kernels, per_device(): pl.pallas_call(functools.partial(exchange, n, ny, lf, wide), out_shape=ja...  89.1 us
    unnamed x16, local copies, waits for them, and re-layouts  23.6 us
    ppermute x4, starting transfers between devices, per_device(): near = [lax.ppermute(xg, 'tensor', perm) for perm in pairs]  9.74 us
  transfers between devices with their start and end apart: 4, of which 0 were waited for; matrix products, arithmetic and copies ran while one was open for 20% of the time, Pallas kernels for 0%

profile of v4, /device:TPU:0, one launch (start us, length us, event | category | flops | bytes accessed | tf_op | source)
XLA Modules:
  0.0 130.5 jit_solution(13601239306122334116)
XLA Ops:
  0.0 0.8 convert_element_type.30
  0.8 1.1 fusion.2.xg
  2.0 0.0 copy-start.2
  2.0 0.5 collective-permute-start.3
  2.5 2.6 %collective-permute-start.2 = (bf16[512,512]{1,0:T(8,128)(2,1)S(1)}, bf16[512,512]{1,0:T(8,128)(2,1)}, u32[]{:S(2)}, u32[]{:S(2)}) collective-permute-start(bf16[512,512]{1,0:T(8,128)(2,1)S(1)} %fusion.2.xg), channel_id=1, source_target_pairs={{0,2},{1,3},{2,0},{3,1},{4,6},{5,7},{6,4},{7,5},{8,10},{9,11},{10,... | collective-permute-start | bytes 1572872 | tf_op jit(solution)/shard_map/ppermute | solution.py:283
  5.1 1.3 collective-permute-start.1
  6.4 5.4 %collective-permute-start = (bf16[512,512]{1,0:T(8,128)(2,1)S(1)}, bf16[512,512]{1,0:T(8,128)(2,1)}, u32[]{:S(2)}, u32[]{:S(2)}) collective-permute-start(bf16[512,512]{1,0:T(8,128)(2,1)S(1)} %fusion.2.xg), channel_id=1, source_target_pairs={{0,4},{1,5},{2,6},{3,7},{4,8},{5,9},{6,10},{7,11},{8,12},{9,13},{1... | collective-permute-start | bytes 1572872 | tf_op jit(solution)/shard_map/ppermute | solution.py:283
  11.8 0.7 copy.23
  12.5 0.2 convert_reduce_fusion
  12.7 0.1 add_bitcast_fusion
  12.8 0.8 select_reduce_fusion
  13.6 0.7 multiply_add_fusion
  14.3 0.4 convolution_convert_fusion
  14.7 0.7 fusion
  15.5 0.2 multiply_reduce_fusion
  15.7 0.4 fusion.5
  16.1 0.8 copy.11.sp
  16.9 20.0 %copy.22 = bf16[8192,2,896]{2,0,1:T(8,128)(2,1)} copy(bf16[8192,2,896]{2,1,0:T(2,128)(2,1)} %param.9) | data formatting | bytes 58720256 | tf_op args[2]
  36.9 0.6 pad.4.ssq
  37.5 0.9 fusion.3.back
  38.4 0.0 collective-permute-done.3.beside
  38.4 0.8 copy-done.4
  39.2 89.1 %shard_map.73 = bf16[512,896]{1,0:T(8,128)(2,1)} custom-call(bf16[512,512]{1,0:T(8,128)(2,1)} %copy-done.2, f32[8,128]{1,0:T(8,128)} %pad.4.ssq, f32[16,32,128]{2,1,0:T(8,128)} %copy.11.sp, bf16[1,2,64,14336]{3,2,1,0:T(8,128)(2,1)} %up.1, bf16[512,512]{1,0:T(8,128)(2,1)} %fusion.3.back, bf16[2,8192,896]{2,1,0:T(8,128)(2,1)} %bitcast.21, ...), custom_call_target="tpu_custom_call" | custom-call | tf_op jit(solution)/shard_map/pallas_call | solution.py:308
  128.3 2.2 %copy.25 = bf16[2,256,896]{2,1,0:T(8,128)(2,1)} copy(bf16[2,256,896]{2,1,0:T(8,128)(2,1)} %bitcast.22) | data formatting | bytes 1835008
  (17 shorter events, 0.1 us)
Async XLA Ops:
  0.0 14.7 %copy-start = (bf16[512,16,128]{2,1,0:T(8,128)(2,1)S(1)}, bf16[512,16,128]{2,1,0:T(8,128)(2,1)}, u32[]{:S(2)}) copy-start(bf16[512,16,128]{2,1,0:T(8,128)(2,1)} %param.10) | copy-start | bytes 6291460
  2.0 13.5 %copy-start.2 = (bf16[512,512]{1,0:T(8,128)(2,1)}, bf16[512,512]{1,0:T(8,128)(2,1)S(1)}, u32[]{:S(2)}) copy-start(bf16[512,512]{1,0:T(8,128)(2,1)S(1)} %fusion.2.xg) | copy-start | bytes 1572868
  2.0 36.4 %collective-permute-start.3 = (bf16[512,512]{1,0:T(8,128)(2,1)S(1)}, bf16[512,512]{1,0:T(8,128)(2,1)S(1)}, u32[]{:S(2)}, u32[]{:S(2)}) collective-permute-start(bf16[512,512]{1,0:T(8,128)(2,1)S(1)} %fusion.2.xg), channel_id=1, source_target_pairs={{0,1},{1,0},{2,3},{3,2},{4,5},{5,4},{6,7},{7,6},{8,9},{9,8},{10,11... | collective-permute-start | bytes 1572872 | tf_op jit(solution)/shard_map/ppermute | solution.py:283
  2.5 35.9 %collective-permute-start.2 = (bf16[512,512]{1,0:T(8,128)(2,1)S(1)}, bf16[512,512]{1,0:T(8,128)(2,1)}, u32[]{:S(2)}, u32[]{:S(2)}) collective-permute-start(bf16[512,512]{1,0:T(8,128)(2,1)S(1)} %fusion.2.xg), channel_id=1, source_target_pairs={{0,2},{1,3},{2,0},{3,1},{4,6},{5,7},{6,4},{7,5},{8,10},{9,11},{10,... | collective-permute-start | bytes 1572872 | tf_op jit(solution)/shard_map/ppermute | solution.py:283
  5.1 33.3 %collective-permute-start.1 = (bf16[512,512]{1,0:T(8,128)(2,1)S(1)}, bf16[512,512]{1,0:T(8,128)(2,1)}, u32[]{:S(2)}, u32[]{:S(2)}) collective-permute-start(bf16[512,512]{1,0:T(8,128)(2,1)S(1)} %fusion.2.xg), channel_id=1, source_target_pairs={{4,0},{5,1},{6,2},{7,3},{8,4},{9,5},{10,6},{11,7},{12,8},{13,9},{1... | collective-permute-start | bytes 1572872 | tf_op jit(solution)/shard_map/ppermute | solution.py:283
  6.4 32.0 %collective-permute-start = (bf16[512,512]{1,0:T(8,128)(2,1)S(1)}, bf16[512,512]{1,0:T(8,128)(2,1)}, u32[]{:S(2)}, u32[]{:S(2)}) collective-permute-start(bf16[512,512]{1,0:T(8,128)(2,1)S(1)} %fusion.2.xg), channel_id=1, source_target_pairs={{0,4},{1,5},{2,6},{3,7},{4,8},{5,9},{6,10},{7,11},{8,12},{9,13},{1... | collective-permute-start | bytes 1572872 | tf_op jit(solution)/shard_map/ppermute | solution.py:283
  14.3 1.2 copy-start.3
  14.3 1.4 %copy-start.5 = (s32[16]{0:T(128)S(1)}, s32[16]{0:T(128)}, u32[]{:S(2)}) copy-start(s32[16]{0:T(128)} %param.13) | copy-start | bytes 196
  38.4 0.8 copy-start.4
  39.2 91.3 %copy-start.1 = (bf16[512,16,128]{2,1,0:T(8,128)(2,1)S(1)}, bf16[512,16,128]{2,1,0:T(8,128)(2,1)}, u32[]{:S(2)}) copy-start(bf16[512,16,128]{2,1,0:T(8,128)(2,1)} %param.10) | copy-start | bytes 6291460

commit v5 on v3

--- a/solution.py
+++ b/solution.py
@@ -157,6 +157,11 @@
         copy.start()
     own[0].wait()
 
+    load.wait()
+    for g in range(2):
+        acc[g] = jnp.dot(xg[...], w[g, pl.ds(pl.multiple_of(me * width, 128), width)],
+                         preferred_element_type=jnp.float32)
+
     @pl.loop(1, n)
     def _(d):
         peer = lax.rem(me + d, n)
@@ -182,11 +187,6 @@
 
     mine = pltpu.make_async_copy(lora_buf.at[me], lora_all.at[me], own_sem.at[3])
     mine.start()
-
-    load.wait()
-    for g in range(2):
-        acc[g] = jnp.dot(xg[...], w[g, pl.ds(pl.multiple_of(me * width, 128), width)],
-                         preferred_element_type=jnp.float32)
 
     use(1, y, core, False)
     use(0, y, 1 - core, False)

time: 126 us -> 126 us (level)
  no operation moved by 1% of the time
where the time goes in v5:
time: 126 us; the launch traced here: 125 us
  Pallas kernels  84 us (67%)
  local copies, waits for them, and re-layouts  25 us (20%)
  starting transfers between devices  9.74 us (8%)
  other arithmetic  4.91 us (4%)
  matrix products  1.58 us (1%)
    pallas_call x1, Pallas kernels, per_device(): pl.pallas_call(functools.partial(exchange, n, ny, lf, wide), out_shape=ja...  84 us
    unnamed x16, local copies, waits for them, and re-layouts  23.6 us
    ppermute x4, starting transfers between devices, per_device(): near = [lax.ppermute(xg, 'tensor', perm) for perm in pairs]  9.74 us
  transfers between devices with their start and end apart: 4, of which 0 were waited for; matrix products, arithmetic and copies ran while one was open for 21% of the time, Pallas kernels for 0%

profile of v5, /device:TPU:0, one launch (start us, length us, event | category | flops | bytes accessed | tf_op | source)
XLA Modules:
  0.0 125.4 jit_solution(13379304291847081309)
XLA Ops:
  0.0 0.8 convert_element_type.30
  0.8 1.1 fusion.2.xg
  2.0 0.0 copy-start.2
  2.0 0.5 collective-permute-start.3
  2.5 2.6 %collective-permute-start.2 = (bf16[512,512]{1,0:T(8,128)(2,1)S(1)}, bf16[512,512]{1,0:T(8,128)(2,1)}, u32[]{:S(2)}, u32[]{:S(2)}) collective-permute-start(bf16[512,512]{1,0:T(8,128)(2,1)S(1)} %fusion.2.xg), channel_id=1, source_target_pairs={{0,2},{1,3},{2,0},{3,1},{4,6},{5,7},{6,4},{7,5},{8,10},{9,11},{10,... | collective-permute-start | bytes 1572872 | tf_op jit(solution)/shard_map/ppermute | solution.py:274
  5.1 1.3 %collective-permute-start.1 = (bf16[512,512]{1,0:T(8,128)(2,1)S(1)}, bf16[512,512]{1,0:T(8,128)(2,1)}, u32[]{:S(2)}, u32[]{:S(2)}) collective-permute-start(bf16[512,512]{1,0:T(8,128)(2,1)S(1)} %fusion.2.xg), channel_id=1, source_target_pairs={{4,0},{5,1},{6,2},{7,3},{8,4},{9,5},{10,6},{11,7},{12,8},{13,9},{1... | collective-permute-start | bytes 1572872 | tf_op jit(solution)/shard_map/ppermute | solution.py:274
  6.4 5.4 %collective-permute-start = (bf16[512,512]{1,0:T(8,128)(2,1)S(1)}, bf16[512,512]{1,0:T(8,128)(2,1)}, u32[]{:S(2)}, u32[]{:S(2)}) collective-permute-start(bf16[512,512]{1,0:T(8,128)(2,1)S(1)} %fusion.2.xg), channel_id=1, source_target_pairs={{0,4},{1,5},{2,6},{3,7},{4,8},{5,9},{6,10},{7,11},{8,12},{9,13},{1... | collective-permute-start | bytes 1572872 | tf_op jit(solution)/shard_map/ppermute | solution.py:274
  11.8 0.7 copy.23
  12.5 0.2 convert_reduce_fusion
  12.7 0.1 add_bitcast_fusion
  12.8 0.8 select_reduce_fusion
  13.6 0.7 multiply_add_fusion
  14.3 0.4 convolution_convert_fusion
  14.7 0.7 fusion
  15.5 0.2 multiply_reduce_fusion
  15.7 0.4 fusion.5
  16.1 0.8 copy.11.sp
  16.9 20.0 %copy.22 = bf16[8192,2,896]{2,0,1:T(8,128)(2,1)} copy(bf16[8192,2,896]{2,1,0:T(2,128)(2,1)} %param.9) | data formatting | bytes 58720256 | tf_op args[2]
  36.9 0.6 pad.4.ssq
  37.5 0.9 fusion.3.back
  38.4 0.0 collective-permute-done.3.beside
  38.4 0.8 copy-done.4
  39.2 84.0 %shard_map.73 = bf16[512,896]{1,0:T(8,128)(2,1)} custom-call(bf16[512,512]{1,0:T(8,128)(2,1)} %copy-done.2, f32[8,128]{1,0:T(8,128)} %pad.4.ssq, f32[16,32,128]{2,1,0:T(8,128)} %copy.11.sp, bf16[1,2,64,14336]{3,2,1,0:T(8,128)(2,1)} %up.1, bf16[512,512]{1,0:T(8,128)(2,1)} %fusion.3.back, bf16[2,8192,896]{2,1,0:T(8,128)(2,1)} %bitcast.21, ...), custom_call_target="tpu_custom_call" | custom-call | tf_op jit(solution)/shard_map/pallas_call | solution.py:299
  123.3 2.2 %copy.25 = bf16[2,256,896]{2,1,0:T(8,128)(2,1)} copy(bf16[2,256,896]{2,1,0:T(8,128)(2,1)} %bitcast.22) | data formatting | bytes 1835008
  (17 shorter events, 0.1 us)
Async XLA Ops:
  0.0 14.7 %copy-start = (bf16[512,16,128]{2,1,0:T(8,128)(2,1)S(1)}, bf16[512,16,128]{2,1,0:T(8,128)(2,1)}, u32[]{:S(2)}) copy-start(bf16[512,16,128]{2,1,0:T(8,128)(2,1)} %param.10) | copy-start | bytes 6291460
  2.0 13.5 %copy-start.2 = (bf16[512,512]{1,0:T(8,128)(2,1)}, bf16[512,512]{1,0:T(8,128)(2,1)S(1)}, u32[]{:S(2)}) copy-start(bf16[512,512]{1,0:T(8,128)(2,1)S(1)} %fusion.2.xg) | copy-start | bytes 1572868
  2.0 36.4 %collective-permute-start.3 = (bf16[512,512]{1,0:T(8,128)(2,1)S(1)}, bf16[512,512]{1,0:T(8,128)(2,1)S(1)}, u32[]{:S(2)}, u32[]{:S(2)}) collective-permute-start(bf16[512,512]{1,0:T(8,128)(2,1)S(1)} %fusion.2.xg), channel_id=1, source_target_pairs={{0,1},{1,0},{2,3},{3,2},{4,5},{5,4},{6,7},{7,6},{8,9},{9,8},{10,11... | collective-permute-start | bytes 1572872 | tf_op jit(solution)/shard_map/ppermute | solution.py:274
  2.5 35.9 %collective-permute-start.2 = (bf16[512,512]{1,0:T(8,128)(2,1)S(1)}, bf16[512,512]{1,0:T(8,128)(2,1)}, u32[]{:S(2)}, u32[]{:S(2)}) collective-permute-start(bf16[512,512]{1,0:T(8,128)(2,1)S(1)} %fusion.2.xg), channel_id=1, source_target_pairs={{0,2},{1,3},{2,0},{3,1},{4,6},{5,7},{6,4},{7,5},{8,10},{9,11},{10,... | collective-permute-start | bytes 1572872 | tf_op jit(solution)/shard_map/ppermute | solution.py:274
  5.1 33.3 %collective-permute-start.1 = (bf16[512,512]{1,0:T(8,128)(2,1)S(1)}, bf16[512,512]{1,0:T(8,128)(2,1)}, u32[]{:S(2)}, u32[]{:S(2)}) collective-permute-start(bf16[512,512]{1,0:T(8,128)(2,1)S(1)} %fusion.2.xg), channel_id=1, source_target_pairs={{4,0},{5,1},{6,2},{7,3},{8,4},{9,5},{10,6},{11,7},{12,8},{13,9},{1... | collective-permute-start | bytes 1572872 | tf_op jit(solution)/shard_map/ppermute | solution.py:274
  6.4 32.0 %collective-permute-start = (bf16[512,512]{1,0:T(8,128)(2,1)S(1)}, bf16[512,512]{1,0:T(8,128)(2,1)}, u32[]{:S(2)}, u32[]{:S(2)}) collective-permute-start(bf16[512,512]{1,0:T(8,128)(2,1)S(1)} %fusion.2.xg), channel_id=1, source_target_pairs={{0,4},{1,5},{2,6},{3,7},{4,8},{5,9},{6,10},{7,11},{8,12},{9,13},{1... | collective-permute-start | bytes 1572872 | tf_op jit(solution)/shard_map/ppermute | solution.py:274
  14.3 1.2 copy-start.3
  14.3 1.4 %copy-start.5 = (s32[16]{0:T(128)S(1)}, s32[16]{0:T(128)}, u32[]{:S(2)}) copy-start(s32[16]{0:T(128)} %param.13) | copy-start | bytes 196
  38.4 0.8 copy-start.4
  39.2 86.2 %copy-start.1 = (bf16[512,16,128]{2,1,0:T(8,128)(2,1)S(1)}, bf16[512,16,128]{2,1,0:T(8,128)(2,1)}, u32[]{:S(2)}) copy-start(bf16[512,16,128]{2,1,0:T(8,128)(2,1)} %param.10) | copy-start | bytes 6291460
